TPU v7x, 512 devices: a whole 4x8x8 slice. The times are simulated.
512 devices in a mesh: rep: 32 (over x, y_hi, core), tp: 8 (over z), seq: 2 (over y_lo).
Axes of the slice: x: 4, y: 8 (y_hi: 4, y_lo: 2; y = y_hi * 2 + y_lo), z: 8, core: 2. Of those that a mesh axis runs over, the one named last changes fastest.
Arguments:
- tokens: bfloat16 [32, 640, 4096], P('rep', 'seq', 'tp'), may hold values from -6 to 6
- queries: bfloat16 [32, 640, 4096], P('rep', 'seq', 'tp'), may hold values from -256 to 256
- output_gradient: bfloat16 [32, 640, 4096], P('rep', 'seq', 'tp'), may hold values from -6 to 6
- key_matrix: bfloat16 [32, 4096, 1024], P('rep', 'seq', 'tp'), may hold values from -0.09375 to 0.09375
- value_matrix: bfloat16 [32, 4096, 1024], P('rep', 'seq', 'tp'), may hold values from -0.09375 to 0.09375
- key_velocity: bfloat16 [32, 4096, 1024], P('rep', 'seq', 'tp'), may hold values from -6 to 6
- value_velocity: bfloat16 [32, 4096, 1024], P('rep', 'seq', 'tp'), may hold values from -6 to 6
- partner_bit: int32 [1], replicated, may hold values from 0 to 1048575
Outputs:
- key_weight_out: bfloat16 [32, 4096, 1024], P('rep', 'seq', 'tp')
- value_weight_out: bfloat16 [32, 4096, 1024], P('rep', 'seq', 'tp')
- key_moment_out: bfloat16 [32, 4096, 1024], P('rep', 'seq', 'tp')
- value_moment_out: bfloat16 [32, 4096, 1024], P('rep', 'seq', 'tp')
All inputs are finite; a program needn't handle non-finite values.
Results may differ from a plain program's by a relative error of at most 0.017.
The roundings to bfloat16 on the way count: a program that leaves them out, or rounds other values in their place, can miss the bound.
Values may be sent and summed in bfloat16 or wider, within the bound.
No kernel may reach another device: no remote copies, remote signals or barrier semaphores. Data moves between devices by JAX's collectives and lax.ppermute only.
A program may use at most 64 MiB of HBM per device.

v0:
```python
import functools
import math

import jax
import jax.numpy as jnp
from jax import lax
from jax.experimental import pallas as pl
from jax.experimental.pallas import tpu as pltpu
from jax.sharding import PartitionSpec as P

HEAD_SIZE = 128
GROUP = 4
PARTS = 4
CROWDED = (1, 2)
MOMENTUM = 0.9
LEARN_RATE = 0.01
SCORE_SCALE = 1.0 / math.sqrt(HEAD_SIZE)
F32 = jnp.float32
BF16 = jnp.bfloat16
VMEM = pl.BlockSpec(memory_space=pltpu.VMEM)
SMEM = pl.BlockSpec(memory_space=pltpu.SMEM)


def nt(a, b):
    return lax.dot_general(a, b, (((1,), (1,)), ((), ())), preferred_element_type=F32)


def tn(a, b):
    return lax.dot_general(a, b, (((0,), (0,)), ((), ())), preferred_element_type=F32)


def nn(a, b):
    return jnp.dot(a, b, preferred_element_type=F32)


def call(kernel, outs, args, scratch=(), flops=0, limit=24):
    moved = sum(math.prod(a.shape) * a.dtype.itemsize for a in (*outs, *args))
    return pl.pallas_call(
        kernel,
        out_shape=outs,
        in_specs=[SMEM] + [VMEM] * (len(args) - 1),
        out_specs=[VMEM] * len(outs),
        scratch_shapes=list(scratch),
        compiler_params=pltpu.CompilerParams(vmem_limit_bytes=limit << 20),
        cost_estimate=pl.CostEstimate(flops=flops, bytes_accessed=moved, transcendentals=0),
    )(*args)


def project_kernel(place, blocks, w_own, w_other, kv_out, x, w, total, x_sem, w_sem):
    count, _, depth = blocks.shape
    half = count // 2
    first = place[0] * half

    def block(i):
        return pltpu.make_async_copy(blocks.at[lax.rem(first + i, count)], x.at[i], x_sem.at[i])

    def rows(side, i):
        at = pl.ds(pl.multiple_of(i * depth, depth), depth)
        source = w_own if side == 0 else w_other
        return pltpu.make_async_copy(source.at[at, :], w.at[side, at, :], w_sem.at[side, i])

    for side in range(2):

        @pl.loop(0, half)
        def _(i):
            rows(side, i).start()
            block(side * half + i).start()

    total[...] = jnp.zeros_like(total)
    for side in range(2):

        @pl.loop(0, half)
        def _(i):
            rows(side, i).wait()
            block(side * half + i).wait()
            part = w[side, pl.ds(pl.multiple_of(i * depth, depth), depth), :]
            total[...] += nn(x[side * half + i], part)

    kv_out[...] = total[...].astype(BF16)


def project(place, blocks, weights, weights_other):
    count, rows, depth = blocks.shape
    features, width = weights.shape
    anywhere = pl.BlockSpec(memory_space=pl.ANY)
    return pl.pallas_call(
        project_kernel,
        out_shape=jax.ShapeDtypeStruct((rows, width), BF16),
        in_specs=[SMEM, anywhere, anywhere, anywhere],
        out_specs=VMEM,
        scratch_shapes=[
            pltpu.VMEM((count, rows, depth), BF16),
            pltpu.VMEM((2, features, width), BF16),
            pltpu.VMEM((rows, width), F32),
            pltpu.SemaphoreType.DMA((count,)),
            pltpu.SemaphoreType.DMA((2, count // 2)),
        ],
        compiler_params=pltpu.CompilerParams(vmem_limit_bytes=56 << 20),
        cost_estimate=pl.CostEstimate(
            flops=2 * rows * count * depth * width, bytes_accessed=2 * rows * count * depth, transcendentals=0
        ),
    )(place, blocks, weights, weights_other)


def attention_kernel(place, q_own, do_own, qdo_other, kv_own, kv_other, d_own, d_other, q_all, do_all, kv_all, d_all):
    seq = place[0]
    other = 1 - seq
    rows = q_own.shape[0]
    width = q_own.shape[1]
    for h in range(GROUP):
        at, col = pl.ds(h * rows, rows), pl.ds(h * HEAD_SIZE, HEAD_SIZE)
        q_all[seq, at, :] = q_own[:, col]
        do_all[seq, at, :] = do_own[:, col]
        q_all[other, at, :] = qdo_other[:, col]
        do_all[other, at, :] = qdo_other[:, pl.ds(width + h * HEAD_SIZE, HEAD_SIZE)]
    kv_all[seq] = kv_own[...]
    kv_all[other] = kv_other[...]
    span = 2 * rows
    key_at = lax.broadcasted_iota(jnp.int32, (rows, span), 0)
    query_at = lax.broadcasted_iota(jnp.int32, (rows, span), 1)
    query_at = jnp.where(query_at >= rows, query_at - rows, query_at)
    causal = key_at <= query_at
    d_all[...] = jnp.zeros_like(d_all)
    for block in range(2):

        @pl.loop(0, GROUP * rows // span)
        def _(chunk):
            at = pl.ds(pl.multiple_of(chunk * span, span), span)
            q = q_all[block, at, :]
            do = do_all[block, at, :]
            scores = []
            for j in range(block + 1):
                s = nt(kv_all[j, :, :HEAD_SIZE], q) * SCORE_SCALE
                scores.append(jnp.where(causal, s, F32(-1e30)) if j == block else s)
            peak = functools.reduce(jnp.maximum, [jnp.max(s, axis=0, keepdims=True) for s in scores])
            weights = [jnp.exp(s - peak) for s in scores]
            share = 1.0 / sum(jnp.sum(e, axis=0, keepdims=True) for e in weights)
            probs = [e * share for e in weights]
            low = [p.astype(BF16) for p in probs]
            grads = [nt(kv_all[j, :, HEAD_SIZE:], do) for j in range(block + 1)]
            dot = sum(jnp.sum(p.astype(F32) * g, axis=0, keepdims=True) for p, g in zip(low, grads))
            for j in range(block + 1):
                score_grad = (probs[j] * (grads[j] - dot)).astype(BF16)
                d_all[j, :, :HEAD_SIZE] += nn(score_grad, q)
                d_all[j, :, HEAD_SIZE:] += nn(low[j], do)

    def reduced(at, out):
        out[:, :HEAD_SIZE] = (d_all[at, :, :HEAD_SIZE] * SCORE_SCALE).astype(BF16)
        out[:, HEAD_SIZE:] = d_all[at, :, HEAD_SIZE:].astype(BF16)

    reduced(seq, d_own)
    reduced(other, d_other)


def moment_kernel(part, place, blocks, x_other, d_own, d_other, key_m, value_m, full, low):
    seq = place[0]
    groups, _, depth = x_other.shape
    first = part * groups

    @pl.loop(0, groups)
    def _(i):
        at = pl.ds(pl.multiple_of(i * depth, depth), depth)
        lines = pl.ds(pl.multiple_of((first + i) * depth, depth), depth)
        own = tn(blocks[seq * (blocks.shape[0] // 2) + first + i], d_own[...])
        far = tn(x_other[i], d_other[...])
        grad = own.astype(BF16).astype(F32) + far.astype(BF16).astype(F32)
        m = jnp.concatenate([key_m[lines, :], value_m[lines, :]], axis=1).astype(F32)
        moment = MOMENTUM * m + grad
        full[at, :] = moment
        low[at, :] = moment.astype(BF16)


def average_kernel(parts, place, w_key, w_value, key_far, value_far, *refs):
    full, far, outs = refs[:parts], refs[parts : 2 * parts], refs[2 * parts :]
    lines, head = full[0].shape[0], w_key.shape[1]
    for part in range(parts):

        @pl.loop(0, lines // head)
        def _(i):
            at = pl.ds(pl.multiple_of(i * head, head), head)
            here = pl.ds(pl.multiple_of(part * lines + i * head, head), head)
            moment = 0.5 * (full[part][at, :] + far[part][at, :].astype(F32))
            for k, (w, w_far) in enumerate(((w_key, key_far), (w_value, value_far))):
                new = moment[:, k * head : (k + 1) * head]
                weight = 0.5 * (w[here, :].astype(F32) + w_far[here, :].astype(F32)) - LEARN_RATE * new
                outs[k][0, here, :] = weight.astype(BF16)
                outs[2 + k][0, here, :] = new.astype(BF16)


def after(block, earlier):
    return lax.optimization_barrier((block, earlier))[0]


def swapped(block, axis, distance):
    return lax.ppermute(block, axis, [(i, i ^ distance) for i in range(lax.axis_size(axis))])


def step(bit, tokens, queries, output_gradient, key_matrix, value_matrix, key_velocity, value_velocity):
    tokens, queries, output_gradient = tokens[0], queries[0], output_gradient[0]
    key_w, value_w, key_m, value_m = key_matrix[0], value_matrix[0], key_velocity[0], value_velocity[0]
    rows, depth = tokens.shape
    features, head = key_w.shape
    crowded = bit in CROWDED
    half = lax.axis_size("tp") // 2
    seq = lax.axis_index("seq")
    place = seq.astype(jnp.int32)[None]
    parts = PARTS
    groups, lines = half // parts, features // parts

    blocks = lax.all_gather(tokens, "tp", axis=0, tiled=False)
    weights = jnp.concatenate([key_w, value_w], axis=1)
    qdo = jnp.concatenate([queries, output_gradient], axis=1)
    weights_other = swapped(weights, "seq", 1)
    qdo_other = swapped(qdo, "seq", 1)
    first = weights_other if crowded else weights
    key_far = swapped(after(key_w, first), "rep", 1 << bit)
    value_far = swapped(after(value_w, first), "rep", 1 << bit)

    shape = jax.ShapeDtypeStruct
    if not crowded:
        blocks, qdo_other, key_far, value_far = lax.optimization_barrier((blocks, qdo_other, key_far, value_far))
    kv = project(place, blocks, weights, weights_other)
    kv_other, qdo_other = lax.optimization_barrier((swapped(kv, "seq", 1), qdo_other))
    if crowded:
        kv_other, key_far = lax.optimization_barrier((kv_other, key_far))
    later = after(blocks, kv_other)
    x_other = []
    for part in range(parts):
        sent = lax.dynamic_slice_in_dim(later, (1 - seq) * half + part * groups, groups, axis=0)
        x_other.append(swapped(sent, "seq", 1))
    wide = pltpu.VMEM((2, GROUP * rows, head), BF16)
    d_own, d_other = call(
        attention_kernel,
        [shape((rows, 2 * head), BF16)] * 2,
        [place, queries, output_gradient, qdo_other, kv, kv_other],
        [wide, wide, pltpu.VMEM((2, rows, 2 * head), BF16), pltpu.VMEM((2, rows, 2 * head), F32)],
        flops=2 * 4 * 3 * GROUP * rows * rows * head,
    )
    if crowded:
        d_own, d_other, value_far = lax.optimization_barrier((d_own, d_other, value_far))
    full, far = [], []
    for part in range(parts):
        moment, low = call(
            functools.partial(moment_kernel, part),
            [shape((lines, 2 * head), F32), shape((lines, 2 * head), BF16)],
            [place, blocks, x_other[part], d_own, d_other, key_m, value_m],
            flops=2 * 2 * rows * lines * 2 * head,
        )
        full.append(moment)
        far.append(swapped(low, "rep", 1 << bit))
    return call(
        functools.partial(average_kernel, parts),
        [shape((1, features, head), BF16)] * 4,
        [place, key_w, value_w, key_far, value_far, *full, *far],
    )


def per_device(*args):
    levels = lax.axis_size("rep").bit_length() - 1
    which = jnp.remainder(args[-1][0], jnp.int32(levels))
    return lax.switch(which, [functools.partial(step, bit) for bit in range(levels)], *args[:-1])


def solution(mesh):
    split = P("rep", "seq", "tp")
    return jax.shard_map(
        per_device,
        mesh=mesh,
        in_specs=(split,) * 7 + (P(),),
        out_specs=(split,) * 4,
        check_vma=False,
    )
```

profile of v0, /device:TPU:1, one launch (start us, length us, event | category | flops | bytes accessed | tf_op | source)
XLA Modules:
  0.0 156.9 jit_solution(8345401213328736586)
XLA Ops:
  7.8 142.2 %conditional.1 = ((bf16[1,2048,128]{2,1,0:T(8,128)(2,1)}, bf16[1,2048,128]{2,1,0:T(8,128)(2,1)}, bf16[1,2048,128]{2,1,0:T(8,128)(2,1)}, bf16[1,2048,128]{2,1,0:T(8,128)(2,1)})) conditional(s32[]{:T(128)} %clamp.3, (bf16[1,2048,128]{2,1,0:T(8,128)(2,1)}, bf16[1,2048,128]{2,1,0:T(8,128)(2,1)}, ...), branch_computations={%region_0.1_spmd, %region_1.2_spmd, %region_2.3_spmd, %region_3.4_... | conditional | flops 2603876352 | bytes 102565032 | solution.py:261
  9.9 4.0 %collective-permute-start.13 = (bf16[2048,256]{1,0:T(8,128)(2,1)S(1)}, bf16[2048,256]{1,0:T(8,128)(2,1)S(1)}, u32[]{:S(2)}, u32[]{:S(2)}) collective-permute-start(bf16[2048,256]{1,0:T(8,128)(2,1)S(1)} %pad_maximum_fusion.2.w_own), channel_id=1, source_target_pairs={{0,1},{1,0},{2,3},{3,2},{4,5},{5,4},{6,7},{7,6},{8,9},{9,8},{10,11... | collective-permute-start | bytes 3145736 | tf_op jit(solution)/shard_map/cond/branch_1_fun/ppermute | solution.py:195
  16.9 15.0 %collective-permute-done.13.w_other = bf16[2048,256]{1,0:T(8,128)(2,1)S(1)} collective-permute-done((bf16[2048,256]{1,0:T(8,128)(2,1)S(1)}, bf16[2048,256]{1,0:T(8,128)(2,1)S(1)}, u32[]{:S(2)}, u32[]{:S(2)}) %collective-permute-start.13) | collective-permute-done | bytes 1048608 | tf_op jit(solution)/shard_map/cond/branch_1_fun/ppermute | solution.py:195
  32.9 9.1 %collective-permute-start.16 = (bf16[2048,128]{1,0:T(8,128)(2,1)}, bf16[2048,128]{1,0:T(8,128)(2,1)S(1)}, u32[]{:S(2)}, u32[]{:S(2)}) collective-permute-start(bf16[2048,128]{1,0:T(8,128)(2,1)} %bitcast.8.w_key), channel_id=1, source_target_pairs={{0,32},{16,48},{32,0},{48,16},{64,96},{80,112},{96,64},{112,80},{1... | collective-permute-start | bytes 1572872 | tf_op jit(solution)/shard_map/cond/branch_1_fun/ppermute | solution.py:195
  42.0 16.8 %all-gather.8.cloned.1.call-done.blocks = bf16[8,320,512]{2,1,0:T(8,128)(2,1)} async-done(((bf16[1,320,512]{2,1,0:T(8,128)(2,1)}), bf16[8,320,512]{2,1,0:T(8,128)(2,1)}) %all-gather.8.cloned.1.call-update) | async-done | bytes 2621456 | tf_op jit(solution)/shard_map/cond/branch_1_fun/all_gather | solution.py:210
  58.8 4.0 %branch_1_fun.7.kv_own = bf16[320,256]{1,0:T(8,128)(2,1)} custom-call(s32[1]{0:T(128)} %bitcast.7.place, bf16[8,320,512]{2,1,0:T(8,128)(2,1)} %all-gather.8.cloned.1.call-done.blocks, bf16[2048,256]{1,0:T(8,128)(2,1)} %copy-done.55, bf16[2048,256]{1,0:T(8,128)(2,1)} %copy-done.57), custom_call_target="tpu_custom_call" | custom-call | flops 671088640 | bytes 2621440 | tf_op jit(solution)/shard_map/cond/branch_1_fun/pallas_call | solution.py:86
  62.9 3.3 %collective-permute-start.14 = (bf16[320,256]{1,0:T(8,128)(2,1)}, bf16[320,256]{1,0:T(8,128)(2,1)S(1)}, u32[]{:S(2)}, u32[]{:S(2)}) collective-permute-start(bf16[320,256]{1,0:T(8,128)(2,1)} %branch_1_fun.7.kv_own), channel_id=1, source_target_pairs={{0,1},{1,0},{2,3},{3,2},{4,5},{5,4},{6,7},{7,6},{8,9},{9,8},{10,11... | collective-permute-start | bytes 491528 | tf_op jit(solution)/shard_map/cond/branch_1_fun/ppermute | solution.py:195
  66.1 4.0 %collective-permute-start.17 = (bf16[2048,128]{1,0:T(8,128)(2,1)}, bf16[2048,128]{1,0:T(8,128)(2,1)}, u32[]{:S(2)}, u32[]{:S(2)}) collective-permute-start(bf16[2048,128]{1,0:T(8,128)(2,1)} %bitcast.9.w_value), channel_id=1, source_target_pairs={{0,32},{16,48},{32,0},{48,16},{64,96},{80,112},{96,64},{112,80},{1... | collective-permute-start | bytes 1572872 | tf_op jit(solution)/shard_map/cond/branch_1_fun/ppermute | solution.py:195
  70.2 2.7 %collective-permute-done.14.kv_other = bf16[320,256]{1,0:T(8,128)(2,1)S(1)} collective-permute-done((bf16[320,256]{1,0:T(8,128)(2,1)}, bf16[320,256]{1,0:T(8,128)(2,1)S(1)}, u32[]{:S(2)}, u32[]{:S(2)}) %collective-permute-start.14) | collective-permute-done | bytes 163872 | tf_op jit(solution)/shard_map/cond/branch_1_fun/ppermute | solution.py:195
  73.0 1.9 %collective-permute-start.18 = (bf16[1,320,512]{2,1,0:T(8,128)(2,1)S(1)}, bf16[1,320,512]{2,1,0:T(8,128)(2,1)S(1)}, u32[]{:S(2)}, u32[]{:S(2)}) collective-permute-start(bf16[1,320,512]{2,1,0:T(8,128)(2,1)S(1)} %get-tuple-element.237), channel_id=1, source_target_pairs={{0,1},{1,0},{2,3},{3,2},{4,5},{5,4},{6,7},{7,6},{8,9},{9,8},{10,11... | collective-permute-start | bytes 983048 | tf_op jit(solution)/shard_map/cond/branch_1_fun/ppermute | solution.py:195
  75.0 3.4 %collective-permute-start.19 = (bf16[1,320,512]{2,1,0:T(8,128)(2,1)S(1)}, bf16[1,320,512]{2,1,0:T(8,128)(2,1)S(1)}, u32[]{:S(2)}, u32[]{:S(2)}) collective-permute-start(bf16[1,320,512]{2,1,0:T(8,128)(2,1)S(1)} %get-tuple-element.236), channel_id=1, source_target_pairs={{0,1},{1,0},{2,3},{3,2},{4,5},{5,4},{6,7},{7,6},{8,9},{9,8},{10,11... | collective-permute-start | bytes 983048 | tf_op jit(solution)/shard_map/cond/branch_1_fun/ppermute | solution.py:195
  78.3 1.9 %collective-permute-start.20 = (bf16[1,320,512]{2,1,0:T(8,128)(2,1)S(1)}, bf16[1,320,512]{2,1,0:T(8,128)(2,1)S(1)}, u32[]{:S(2)}, u32[]{:S(2)}) collective-permute-start(bf16[1,320,512]{2,1,0:T(8,128)(2,1)S(1)} %get-tuple-element.235), channel_id=1, source_target_pairs={{0,1},{1,0},{2,3},{3,2},{4,5},{5,4},{6,7},{7,6},{8,9},{9,8},{10,11... | collective-permute-start | bytes 983048 | tf_op jit(solution)/shard_map/cond/branch_1_fun/ppermute | solution.py:195
  80.3 3.7 %collective-permute-start.21 = (bf16[1,320,512]{2,1,0:T(8,128)(2,1)S(1)}, bf16[1,320,512]{2,1,0:T(8,128)(2,1)S(1)}, u32[]{:S(2)}, u32[]{:S(2)}) collective-permute-start(bf16[1,320,512]{2,1,0:T(8,128)(2,1)S(1)} %get-tuple-element.234), channel_id=1, source_target_pairs={{0,1},{1,0},{2,3},{3,2},{4,5},{5,4},{6,7},{7,6},{8,9},{9,8},{10,11... | collective-permute-start | bytes 983048 | tf_op jit(solution)/shard_map/cond/branch_1_fun/ppermute | solution.py:195
  84.0 6.6 %branch_1_fun.8 = (bf16[320,256]{1,0:T(8,128)(2,1)S(1)}, bf16[320,256]{1,0:T(8,128)(2,1)S(1)}) custom-call(s32[1]{0:T(128)} %bitcast.7.place, bf16[320,512]{1,0:T(8,128)(2,1)S(1)} %bitcast.79, bf16[320,512]{1,0:T(8,128)(2,1)S(1)} %bitcast.89, bf16[320,1024]{1,0:T(8,128)(2,1)} %collective-permute-done.15.qdo_other, bf16[320,256]{1,0:T(8,128)(2,1)S(1)} %copy-done.11, ...), custom_call_target="tpu_custom_call" | custom-call | flops 1258291200 | bytes 1966084 | tf_op jit(solution)/shard_map/cond/branch_1_fun/pallas_call | solution.py:38
  90.6 2.5 %collective-permute-done.17.value_far = bf16[2048,128]{1,0:T(8,128)(2,1)} collective-permute-done((bf16[2048,128]{1,0:T(8,128)(2,1)}, bf16[2048,128]{1,0:T(8,128)(2,1)}, u32[]{:S(2)}, u32[]{:S(2)}) %collective-permute-start.17) | collective-permute-done | bytes 524320 | tf_op jit(solution)/shard_map/cond/branch_1_fun/ppermute | solution.py:195
  93.6 1.9 %collective-permute-start.22 = (bf16[512,256]{1,0:T(8,128)(2,1)S(1)}, bf16[512,256]{1,0:T(8,128)(2,1)S(1)}, u32[]{:S(2)}, u32[]{:S(2)}) collective-permute-start(bf16[512,256]{1,0:T(8,128)(2,1)S(1)} %get-tuple-element.119), channel_id=1, source_target_pairs={{0,32},{16,48},{32,0},{48,16},{64,96},{80,112},{96,64},{112,80},{1... | collective-permute-start | bytes 786440 | tf_op jit(solution)/shard_map/cond/branch_1_fun/ppermute | solution.py:195
  95.5 2.4 %collective-permute-done.19.x_other = bf16[1,320,512]{2,1,0:T(8,128)(2,1)S(1)} collective-permute-done((bf16[1,320,512]{2,1,0:T(8,128)(2,1)S(1)}, bf16[1,320,512]{2,1,0:T(8,128)(2,1)S(1)}, u32[]{:S(2)}, u32[]{:S(2)}) %collective-permute-start.19) | collective-permute-done | bytes 327712 | tf_op jit(solution)/shard_map/cond/branch_1_fun/ppermute | solution.py:195
  98.5 1.9 %collective-permute-start.23 = (bf16[512,256]{1,0:T(8,128)(2,1)S(1)}, bf16[512,256]{1,0:T(8,128)(2,1)S(1)}, u32[]{:S(2)}, u32[]{:S(2)}) collective-permute-start(bf16[512,256]{1,0:T(8,128)(2,1)S(1)} %get-tuple-element.120), channel_id=1, source_target_pairs={{0,32},{16,48},{32,0},{48,16},{64,96},{80,112},{96,64},{112,80},{1... | collective-permute-start | bytes 786440 | tf_op jit(solution)/shard_map/cond/branch_1_fun/ppermute | solution.py:195
  100.4 13.0 %collective-permute-done.20.x_other = bf16[1,320,512]{2,1,0:T(8,128)(2,1)S(1)} collective-permute-done((bf16[1,320,512]{2,1,0:T(8,128)(2,1)S(1)}, bf16[1,320,512]{2,1,0:T(8,128)(2,1)S(1)}, u32[]{:S(2)}, u32[]{:S(2)}) %collective-permute-start.20) | collective-permute-done | bytes 327712 | tf_op jit(solution)/shard_map/cond/branch_1_fun/ppermute | solution.py:195
  113.9 1.9 %collective-permute-start.24 = (bf16[512,256]{1,0:T(8,128)(2,1)S(1)}, bf16[512,256]{1,0:T(8,128)(2,1)S(1)}, u32[]{:S(2)}, u32[]{:S(2)}) collective-permute-start(bf16[512,256]{1,0:T(8,128)(2,1)S(1)} %get-tuple-element.121), channel_id=1, source_target_pairs={{0,32},{16,48},{32,0},{48,16},{64,96},{80,112},{96,64},{112,80},{1... | collective-permute-start | bytes 786440 | tf_op jit(solution)/shard_map/cond/branch_1_fun/ppermute | solution.py:195
  115.8 4.7 %collective-permute-done.21.x_other = bf16[1,320,512]{2,1,0:T(8,128)(2,1)S(1)} collective-permute-done((bf16[1,320,512]{2,1,0:T(8,128)(2,1)S(1)}, bf16[1,320,512]{2,1,0:T(8,128)(2,1)S(1)}, u32[]{:S(2)}, u32[]{:S(2)}) %collective-permute-start.21) | collective-permute-done | bytes 327712 | tf_op jit(solution)/shard_map/cond/branch_1_fun/ppermute | solution.py:195
  123.0 18.0 %collective-permute-done.24.refs_6_ = bf16[512,256]{1,0:T(8,128)(2,1)S(1)} collective-permute-done((bf16[512,256]{1,0:T(8,128)(2,1)S(1)}, bf16[512,256]{1,0:T(8,128)(2,1)S(1)}, u32[]{:S(2)}, u32[]{:S(2)}) %collective-permute-start.24) | collective-permute-done | bytes 262176 | tf_op jit(solution)/shard_map/cond/branch_1_fun/ppermute | solution.py:195
  141.0 5.6 %collective-permute-done.25.refs_7_ = bf16[512,256]{1,0:T(8,128)(2,1)S(1)} collective-permute-done((bf16[512,256]{1,0:T(8,128)(2,1)S(1)}, bf16[512,256]{1,0:T(8,128)(2,1)S(1)}, u32[]{:S(2)}, u32[]{:S(2)}) %collective-permute-start.25) | collective-permute-done | bytes 262176 | tf_op jit(solution)/shard_map/cond/branch_1_fun/ppermute | solution.py:195
  146.6 3.4 %branch_1_fun.13 = (bf16[1,2048,128]{2,1,0:T(8,128)(2,1)}, bf16[1,2048,128]{2,1,0:T(8,128)(2,1)}, bf16[1,2048,128]{2,1,0:T(8,128)(2,1)}, bf16[1,2048,128]{2,1,0:T(8,128)(2,1)}) custom-call(s32[1]{0:T(128)} %bitcast.7.place, bf16[2048,128]{1,0:T(8,128)(2,1)} %bitcast.8.w_key, bf16[2048,128]{1,0:T(8,128)(2,1)} %bitcast.9.w_value, ...), custom_call_target="tpu_custom_call" | custom-call | bytes 7340036 | tf_op jit(solution)/shard_map/cond/branch_1_fun/pallas_call | solution.py:38
  (36 shorter events, 10.0 us)
Async XLA Ops:
  7.9 6.1 %copy-start.34 = (bf16[1,320,512]{2,1,0:T(8,128)(2,1)S(1)}, bf16[1,320,512]{2,1,0:T(8,128)(2,1)}, u32[]{:S(2)}) copy-start(bf16[1,320,512]{2,1,0:T(8,128)(2,1)} %get-tuple-element.99) | copy-start | bytes 983044 | tf_op jit(solution)/shard_map/cond
  7.9 6.1 %copy-start.44 = (bf16[1,320,512]{2,1,0:T(8,128)(2,1)S(1)}, bf16[1,320,512]{2,1,0:T(8,128)(2,1)}, u32[]{:S(2)}) copy-start(bf16[1,320,512]{2,1,0:T(8,128)(2,1)} %get-tuple-element.100) | copy-start | bytes 983044 | tf_op jit(solution)/shard_map/cond
  7.9 50.9 %all-gather.8.cloned.1.call-start = ((), (), s32[]{:S(2)}) async-start(), calls=%async_computation.1 | async-start | bytes 2949120 | tf_op jit(solution)/shard_map/cond/branch_1_fun/all_gather | solution.py:210
  9.9 7.0 %copy-start.55 = (bf16[2048,256]{1,0:T(8,128)(2,1)}, bf16[2048,256]{1,0:T(8,128)(2,1)S(1)}, u32[]{:S(2)}) copy-start(bf16[2048,256]{1,0:T(8,128)(2,1)S(1)} %pad_maximum_fusion.2.w_own) | copy-start | bytes 3145732 | tf_op jit(solution)/shard_map/cond
  9.9 22.0 %collective-permute-start.13 = (bf16[2048,256]{1,0:T(8,128)(2,1)S(1)}, bf16[2048,256]{1,0:T(8,128)(2,1)S(1)}, u32[]{:S(2)}, u32[]{:S(2)}) collective-permute-start(bf16[2048,256]{1,0:T(8,128)(2,1)S(1)} %pad_maximum_fusion.2.w_own), channel_id=1, source_target_pairs={{0,1},{1,0},{2,3},{3,2},{4,5},{5,4},{6,7},{7,6},{8,9},{9,8},{10,11... | collective-permute-start | bytes 3145736 | tf_op jit(solution)/shard_map/cond/branch_1_fun/ppermute | solution.py:195
  15.0 55.2 %collective-permute-start.15 = (bf16[320,1024]{1,0:T(8,128)(2,1)}, bf16[320,1024]{1,0:T(8,128)(2,1)}, u32[]{:S(2)}, u32[]{:S(2)}) collective-permute-start(bf16[320,1024]{1,0:T(8,128)(2,1)} %pad_maximum_fusion.3), channel_id=1, source_target_pairs={{0,1},{1,0},{2,3},{3,2},{4,5},{5,4},{6,7},{7,6},{8,9},{9,8},{10,11... | collective-permute-start | bytes 1966088 | tf_op jit(solution)/shard_map/cond/branch_1_fun/ppermute | solution.py:195
  31.9 1.0 copy-start.57
  32.9 40.0 %collective-permute-start.16 = (bf16[2048,128]{1,0:T(8,128)(2,1)}, bf16[2048,128]{1,0:T(8,128)(2,1)S(1)}, u32[]{:S(2)}, u32[]{:S(2)}) collective-permute-start(bf16[2048,128]{1,0:T(8,128)(2,1)} %bitcast.8.w_key), channel_id=1, source_target_pairs={{0,32},{16,48},{32,0},{48,16},{64,96},{80,112},{96,64},{112,80},{1... | collective-permute-start | bytes 1572872 | tf_op jit(solution)/shard_map/cond/branch_1_fun/ppermute | solution.py:195
  58.8 14.1 %copy-start.1 = (bf16[8,320,512]{2,1,0:T(8,128)(2,1)S(1)}, bf16[8,320,512]{2,1,0:T(8,128)(2,1)}, u32[]{:S(2)}) copy-start(bf16[8,320,512]{2,1,0:T(8,128)(2,1)} %all-gather.8.cloned.1.call-done.blocks) | copy-start | bytes 7864324 | tf_op jit(solution)/shard_map/cond
  62.8 21.1 %copy-start.11 = (bf16[320,256]{1,0:T(8,128)(2,1)S(1)}, bf16[320,256]{1,0:T(8,128)(2,1)}, u32[]{:S(2)}) copy-start(bf16[320,256]{1,0:T(8,128)(2,1)} %branch_1_fun.7.kv_own) | copy-start | bytes 491524 | tf_op jit(solution)/shard_map/cond
  62.9 10.1 %collective-permute-start.14 = (bf16[320,256]{1,0:T(8,128)(2,1)}, bf16[320,256]{1,0:T(8,128)(2,1)S(1)}, u32[]{:S(2)}, u32[]{:S(2)}) collective-permute-start(bf16[320,256]{1,0:T(8,128)(2,1)} %branch_1_fun.7.kv_own), channel_id=1, source_target_pairs={{0,1},{1,0},{2,3},{3,2},{4,5},{5,4},{6,7},{7,6},{8,9},{9,8},{10,11... | collective-permute-start | bytes 491528 | tf_op jit(solution)/shard_map/cond/branch_1_fun/ppermute | solution.py:195
  66.1 27.0 %collective-permute-start.17 = (bf16[2048,128]{1,0:T(8,128)(2,1)}, bf16[2048,128]{1,0:T(8,128)(2,1)}, u32[]{:S(2)}, u32[]{:S(2)}) collective-permute-start(bf16[2048,128]{1,0:T(8,128)(2,1)} %bitcast.9.w_value), channel_id=1, source_target_pairs={{0,32},{16,48},{32,0},{48,16},{64,96},{80,112},{96,64},{112,80},{1... | collective-permute-start | bytes 1572872 | tf_op jit(solution)/shard_map/cond/branch_1_fun/ppermute | solution.py:195
  70.2 13.8 %copy-start.35 = (bf16[1,320,512]{2,1,0:T(8,128)(2,1)S(1)}, bf16[1,320,512]{2,1,0:T(8,128)(2,1)}, u32[]{:S(2)}) copy-start(bf16[1,320,512]{2,1,0:T(8,128)(2,1)} %get-tuple-element.99) | copy-start | bytes 983044 | tf_op jit(solution)/shard_map/cond
  70.2 13.8 %copy-start.45 = (bf16[1,320,512]{2,1,0:T(8,128)(2,1)S(1)}, bf16[1,320,512]{2,1,0:T(8,128)(2,1)}, u32[]{:S(2)}) copy-start(bf16[1,320,512]{2,1,0:T(8,128)(2,1)} %get-tuple-element.100) | copy-start | bytes 983044 | tf_op jit(solution)/shard_map/cond
  73.0 20.1 %collective-permute-start.18 = (bf16[1,320,512]{2,1,0:T(8,128)(2,1)S(1)}, bf16[1,320,512]{2,1,0:T(8,128)(2,1)S(1)}, u32[]{:S(2)}, u32[]{:S(2)}) collective-permute-start(bf16[1,320,512]{2,1,0:T(8,128)(2,1)S(1)} %get-tuple-element.237), channel_id=1, source_target_pairs={{0,1},{1,0},{2,3},{3,2},{4,5},{5,4},{6,7},{7,6},{8,9},{9,8},{10,11... | collective-permute-start | bytes 983048 | tf_op jit(solution)/shard_map/cond/branch_1_fun/ppermute | solution.py:195
  75.0 23.0 %collective-permute-start.19 = (bf16[1,320,512]{2,1,0:T(8,128)(2,1)S(1)}, bf16[1,320,512]{2,1,0:T(8,128)(2,1)S(1)}, u32[]{:S(2)}, u32[]{:S(2)}) collective-permute-start(bf16[1,320,512]{2,1,0:T(8,128)(2,1)S(1)} %get-tuple-element.236), channel_id=1, source_target_pairs={{0,1},{1,0},{2,3},{3,2},{4,5},{5,4},{6,7},{7,6},{8,9},{9,8},{10,11... | collective-permute-start | bytes 983048 | tf_op jit(solution)/shard_map/cond/branch_1_fun/ppermute | solution.py:195
  78.3 35.1 %collective-permute-start.20 = (bf16[1,320,512]{2,1,0:T(8,128)(2,1)S(1)}, bf16[1,320,512]{2,1,0:T(8,128)(2,1)S(1)}, u32[]{:S(2)}, u32[]{:S(2)}) collective-permute-start(bf16[1,320,512]{2,1,0:T(8,128)(2,1)S(1)} %get-tuple-element.235), channel_id=1, source_target_pairs={{0,1},{1,0},{2,3},{3,2},{4,5},{5,4},{6,7},{7,6},{8,9},{9,8},{10,11... | collective-permute-start | bytes 983048 | tf_op jit(solution)/shard_map/cond/branch_1_fun/ppermute | solution.py:195
  80.3 12.9 %copy-start.23 = (bf16[1,2048,128]{2,1,0:T(8,128)(2,1)S(1)}, bf16[1,2048,128]{2,1,0:T(8,128)(2,1)}, u32[]{:S(2)}) copy-start(bf16[1,2048,128]{2,1,0:T(8,128)(2,1)} %get-tuple-element.113) | copy-start | bytes 1572868 | tf_op jit(solution)/shard_map/cond
  80.3 12.8 %copy-start.28 = (bf16[1,2048,128]{2,1,0:T(8,128)(2,1)S(1)}, bf16[1,2048,128]{2,1,0:T(8,128)(2,1)}, u32[]{:S(2)}) copy-start(bf16[1,2048,128]{2,1,0:T(8,128)(2,1)} %get-tuple-element.114) | copy-start | bytes 1572868 | tf_op jit(solution)/shard_map/cond
  80.3 40.2 %collective-permute-start.21 = (bf16[1,320,512]{2,1,0:T(8,128)(2,1)S(1)}, bf16[1,320,512]{2,1,0:T(8,128)(2,1)S(1)}, u32[]{:S(2)}, u32[]{:S(2)}) collective-permute-start(bf16[1,320,512]{2,1,0:T(8,128)(2,1)S(1)} %get-tuple-element.234), channel_id=1, source_target_pairs={{0,1},{1,0},{2,3},{3,2},{4,5},{5,4},{6,7},{7,6},{8,9},{9,8},{10,11... | collective-permute-start | bytes 983048 | tf_op jit(solution)/shard_map/cond/branch_1_fun/ppermute | solution.py:195
  93.6 29.3 %collective-permute-start.22 = (bf16[512,256]{1,0:T(8,128)(2,1)S(1)}, bf16[512,256]{1,0:T(8,128)(2,1)S(1)}, u32[]{:S(2)}, u32[]{:S(2)}) collective-permute-start(bf16[512,256]{1,0:T(8,128)(2,1)S(1)} %get-tuple-element.119), channel_id=1, source_target_pairs={{0,32},{16,48},{32,0},{48,16},{64,96},{80,112},{96,64},{112,80},{1... | collective-permute-start | bytes 786440 | tf_op jit(solution)/shard_map/cond/branch_1_fun/ppermute | solution.py:195
  98.5 24.5 %collective-permute-start.23 = (bf16[512,256]{1,0:T(8,128)(2,1)S(1)}, bf16[512,256]{1,0:T(8,128)(2,1)S(1)}, u32[]{:S(2)}, u32[]{:S(2)}) collective-permute-start(bf16[512,256]{1,0:T(8,128)(2,1)S(1)} %get-tuple-element.120), channel_id=1, source_target_pairs={{0,32},{16,48},{32,0},{48,16},{64,96},{80,112},{96,64},{112,80},{1... | collective-permute-start | bytes 786440 | tf_op jit(solution)/shard_map/cond/branch_1_fun/ppermute | solution.py:195
  113.9 27.1 %collective-permute-start.24 = (bf16[512,256]{1,0:T(8,128)(2,1)S(1)}, bf16[512,256]{1,0:T(8,128)(2,1)S(1)}, u32[]{:S(2)}, u32[]{:S(2)}) collective-permute-start(bf16[512,256]{1,0:T(8,128)(2,1)S(1)} %get-tuple-element.121), channel_id=1, source_target_pairs={{0,32},{16,48},{32,0},{48,16},{64,96},{80,112},{96,64},{112,80},{1... | collective-permute-start | bytes 786440 | tf_op jit(solution)/shard_map/cond/branch_1_fun/ppermute | solution.py:195
  121.0 25.6 %collective-permute-start.25 = (bf16[512,256]{1,0:T(8,128)(2,1)S(1)}, bf16[512,256]{1,0:T(8,128)(2,1)S(1)}, u32[]{:S(2)}, u32[]{:S(2)}) collective-permute-start(bf16[512,256]{1,0:T(8,128)(2,1)S(1)} %get-tuple-element.122), channel_id=1, source_target_pairs={{0,32},{16,48},{32,0},{48,16},{64,96},{80,112},{96,64},{112,80},{1... | collective-permute-start | bytes 786440 | tf_op jit(solution)/shard_map/cond/branch_1_fun/ppermute | solution.py:195
Sparse Core Ops, SparseCore 0:
  10.8 47.9 all-gather.7
where the time goes:
time: 159 us; the launch traced here: 157 us
  waiting for transfers between devices  81.5 us (51%)
  starting transfers between devices  40.9 us (26%)
  Pallas kernels  16 us (10%)
  between operations  14.7 us (9%)
  other arithmetic  2.33 us (1%)
    ppermute x13, waiting for transfers between devices, swapped(): lax.ppermute(block, axis, [(i, i ^ distance) for i in range(lax.axis_size...  64 us
    ppermute x13, starting transfers between devices, swapped(): lax.ppermute(block, axis, [(i, i ^ distance) for i in range(lax.axis_size...  40.9 us
    all_gather x1, waiting for transfers between devices, step(): blocks = lax.all_gather(tokens, 'tp', axis=0, tiled=False)  16.8 us
    pallas_call x6, Pallas kernels, call(): pl.pallas_call(kernel, out_shape=outs, in_specs=[SMEM] + [VMEM] * (len(ar...  12 us
    pallas_call x1, Pallas kernels, project(): pl.pallas_call(project_kernel, out_shape=jax.ShapeDtypeStruct((rows, widt...  4.01 us
  transfers between devices with their start and end apart: 14, of which 9 were waited for; matrix products, arithmetic and copies ran while one was open for 2% of the time, Pallas kernels for 8%

commit v1 on v0

--- a/solution.py
+++ b/solution.py
@@ -10,7 +10,7 @@
 
 HEAD_SIZE = 128
 GROUP = 4
-PARTS = 4
+FAR = (2,)
 CROWDED = (1, 2)
 MOMENTUM = 0.9
 LEARN_RATE = 0.01
@@ -152,25 +152,23 @@
     reduced(other, d_other)
 
 
-def moment_kernel(part, place, blocks, x_other, d_own, d_other, key_m, value_m, full, low):
-    seq = place[0]
-    groups, _, depth = x_other.shape
-    first = part * groups
-
-    @pl.loop(0, groups)
-    def _(i):
-        at = pl.ds(pl.multiple_of(i * depth, depth), depth)
-        lines = pl.ds(pl.multiple_of((first + i) * depth, depth), depth)
-        own = tn(blocks[seq * (blocks.shape[0] // 2) + first + i], d_own[...])
-        far = tn(x_other[i], d_other[...])
+def moment_kernel(group, entry, place, blocks, x_other, d_own, d_other, key_m, value_m, full, low):
+    group = place[entry] if group is None else group
+    depth = blocks.shape[2]
+
+    @pl.loop(0, 1)
+    def _(_):
+        own = tn(blocks[place[0] * (blocks.shape[0] // 2) + group], d_own[...])
+        far = tn(x_other[0], d_other[...])
         grad = own.astype(BF16).astype(F32) + far.astype(BF16).astype(F32)
+        lines = pl.ds(pl.multiple_of(group * depth, depth), depth)
         m = jnp.concatenate([key_m[lines, :], value_m[lines, :]], axis=1).astype(F32)
         moment = MOMENTUM * m + grad
-        full[at, :] = moment
-        low[at, :] = moment.astype(BF16)
-
-
-def average_kernel(parts, place, w_key, w_value, key_far, value_far, *refs):
+        full[...] = moment
+        low[...] = moment.astype(BF16)
+
+
+def average_kernel(parts, moved, place, w_key, w_value, key_far, value_far, *refs):
     full, far, outs = refs[:parts], refs[parts : 2 * parts], refs[2 * parts :]
     lines, head = full[0].shape[0], w_key.shape[1]
     for part in range(parts):
@@ -178,7 +176,8 @@
         @pl.loop(0, lines // head)
         def _(i):
             at = pl.ds(pl.multiple_of(i * head, head), head)
-            here = pl.ds(pl.multiple_of(part * lines + i * head, head), head)
+            group = place[1 + part] if moved else part
+            here = pl.ds(pl.multiple_of(group * lines + i * head, head), head)
             moment = 0.5 * (full[part][at, :] + far[part][at, :].astype(F32))
             for k, (w, w_far) in enumerate(((w_key, key_far), (w_value, value_far))):
                 new = moment[:, k * head : (k + 1) * head]
@@ -191,6 +190,11 @@
     return lax.optimization_barrier((block, earlier))[0]
 
 
+def shifted(block, distance):
+    count = lax.axis_size("tp")
+    return lax.ppermute(block, "tp", [(i, (i + distance) % count) for i in range(count)])
+
+
 def swapped(block, axis, distance):
     return lax.ppermute(block, axis, [(i, i ^ distance) for i in range(lax.axis_size(axis))])
 
@@ -201,11 +205,12 @@
     rows, depth = tokens.shape
     features, head = key_w.shape
     crowded = bit in CROWDED
+    far_apart = bit in FAR
     half = lax.axis_size("tp") // 2
-    seq = lax.axis_index("seq")
-    place = seq.astype(jnp.int32)[None]
-    parts = PARTS
-    groups, lines = half // parts, features // parts
+    seq, tp = lax.axis_index("seq"), lax.axis_index("tp")
+    order = [jnp.remainder(tp + k + half, half) for k in (0, -1, 1, -2)] if far_apart else list(range(half))
+    place = (jnp.stack([seq, *order]) if far_apart else seq[None]).astype(jnp.int32)
+    lines = features // half
 
     blocks = lax.all_gather(tokens, "tp", axis=0, tiled=False)
     weights = jnp.concatenate([key_w, value_w], axis=1)
@@ -214,7 +219,8 @@
     qdo_other = swapped(qdo, "seq", 1)
     first = weights_other if crowded else weights
     key_far = swapped(after(key_w, first), "rep", 1 << bit)
-    value_far = swapped(after(value_w, first), "rep", 1 << bit)
+    if not far_apart:
+        value_far = swapped(after(value_w, first), "rep", 1 << bit)
 
     shape = jax.ShapeDtypeStruct
     if not crowded:
@@ -225,9 +231,11 @@
         kv_other, key_far = lax.optimization_barrier((kv_other, key_far))
     later = after(blocks, kv_other)
     x_other = []
-    for part in range(parts):
-        sent = lax.dynamic_slice_in_dim(later, (1 - seq) * half + part * groups, groups, axis=0)
+    for group in order[:1] if far_apart else order:
+        sent = lax.dynamic_slice_in_dim(later, (1 - seq) * half + group, 1, axis=0)
         x_other.append(swapped(sent, "seq", 1))
+    if far_apart:
+        value_far = swapped(after(value_w, x_other[0]), "rep", 1 << bit)
     wide = pltpu.VMEM((2, GROUP * rows, head), BF16)
     d_own, d_other = call(
         attention_kernel,
@@ -236,12 +244,17 @@
         [wide, wide, pltpu.VMEM((2, rows, 2 * head), BF16), pltpu.VMEM((2, rows, 2 * head), F32)],
         flops=2 * 4 * 3 * GROUP * rows * rows * head,
     )
-    if crowded:
+    if far_apart:
+        near = after(x_other[0], d_own)
+        x_other += [shifted(near, 1), shifted(near, -1)]
+        x_other.append(shifted(x_other[1], 1))
+        x_other[3], value_far = lax.optimization_barrier((x_other[3], value_far))
+    elif crowded:
         d_own, d_other, value_far = lax.optimization_barrier((d_own, d_other, value_far))
     full, far = [], []
-    for part in range(parts):
+    for part in range(half):
         moment, low = call(
-            functools.partial(moment_kernel, part),
+            functools.partial(moment_kernel, None if far_apart else order[part], 1 + part),
             [shape((lines, 2 * head), F32), shape((lines, 2 * head), BF16)],
             [place, blocks, x_other[part], d_own, d_other, key_m, value_m],
             flops=2 * 2 * rows * lines * 2 * head,
@@ -249,7 +262,7 @@
         full.append(moment)
         far.append(swapped(low, "rep", 1 << bit))
     return call(
-        functools.partial(average_kernel, parts),
+        functools.partial(average_kernel, half, far_apart),
         [shape((1, features, head), BF16)] * 4,
         [place, key_w, value_w, key_far, value_far, *full, *far],
     )

time: 159 us -> 117 us (0.74)
  waiting for transfers between devices: 81.5 us -> 35.4 us
  starting transfers between devices: 40.9 us -> 47.6 us
    ppermute x13, waiting for transfers between devices: 64 us -> 22.7 us  [swapped(): lax.ppermute(block, axis, [(i, i ^ distance) for i in range(lax.axis_size...]
    ppermute x13, starting transfers between devices: 40.9 us -> 47.6 us  [swapped(): lax.ppermute(block, axis, [(i, i ^ distance) for i in range(lax.axis_size...]
    all_gather x1, waiting for transfers between devices: 16.8 us -> 12 us  [step(): blocks = lax.all_gather(tokens, 'tp', axis=0, tiled=False)]
  transfers between devices with their start and end apart: 14 -> 14, of which waited for: 9 -> 5; matrix products, arithmetic and copies ran while one was open for 2% -> 1% of each run, Pallas kernels for 8% -> 6%
where the time goes in v1:
time: 117 us; the launch traced here: 116 us
  starting transfers between devices  47.6 us (41%)
  waiting for transfers between devices  35.4 us (30%)
  Pallas kernels  14.8 us (13%)
  between operations  14.7 us (13%)
  local copies, waits for them, and re-layouts  1.78 us (2%)
  other arithmetic  1.39 us (1%)
    ppermute x13, starting transfers between devices, swapped(): lax.ppermute(block, axis, [(i, i ^ distance) for i in range(lax.axis_size...  47.6 us
    ppermute x13, waiting for transfers between devices, swapped(): lax.ppermute(block, axis, [(i, i ^ distance) for i in range(lax.axis_size...  22.7 us
    all_gather x1, waiting for transfers between devices, step(): blocks = lax.all_gather(tokens, 'tp', axis=0, tiled=False)  12 us
    pallas_call x6, Pallas kernels, call(): pl.pallas_call(kernel, out_shape=outs, in_specs=[SMEM] + [VMEM] * (len(ar...  10.8 us
    pallas_call x1, Pallas kernels, project(): pl.pallas_call(project_kernel, out_shape=jax.ShapeDtypeStruct((rows, widt...  4 us
  transfers between devices with their start and end apart: 14, of which 5 were waited for; matrix products, arithmetic and copies ran while one was open for 1% of the time, Pallas kernels for 6%

profile of v1, /device:TPU:1, one launch (start us, length us, event | category | flops | bytes accessed | tf_op | source)
XLA Modules:
  0.0 116.1 jit_solution(2208876246403259632)
XLA Ops:
  7.8 101.4 %conditional.1 = ((bf16[1,2048,128]{2,1,0:T(8,128)(2,1)}, bf16[1,2048,128]{2,1,0:T(8,128)(2,1)}, bf16[1,2048,128]{2,1,0:T(8,128)(2,1)}, bf16[1,2048,128]{2,1,0:T(8,128)(2,1)})) conditional(s32[]{:T(128)} %clamp.3, (bf16[1,2048,128]{2,1,0:T(8,128)(2,1)}, bf16[1,2048,128]{2,1,0:T(8,128)(2,1)}, ...), branch_computations={%region_0.1_spmd, %region_1.2_spmd, %region_2.3_spmd, %region_3.4_... | conditional | flops 2603876352 | bytes 102565032 | solution.py:274
  8.6 1.3 %pad_maximum_fusion.w_own = bf16[2048,256]{1,0:T(8,128)(2,1)S(1)} fusion(bf16[2048,128]{1,0:T(8,128)(2,1)} %bitcast.2.w_value, bf16[2048,128]{1,0:T(8,128)(2,1)} %bitcast.1.w_key), kind=kLoop, calls=%fused_computation | loop fusion | flops 2097152 | bytes 2097152 | tf_op jit(solution)/shard_map/cond/branch_0_fun/concatenate | solution.py:216
  9.9 4.0 %collective-permute-start.3 = (bf16[2048,256]{1,0:T(8,128)(2,1)S(1)}, bf16[2048,256]{1,0:T(8,128)(2,1)}, u32[]{:S(2)}, u32[]{:S(2)}) collective-permute-start(bf16[2048,256]{1,0:T(8,128)(2,1)S(1)} %pad_maximum_fusion.w_own), channel_id=1, source_target_pairs={{0,1},{1,0},{2,3},{3,2},{4,5},{5,4},{6,7},{7,6},{8,9},{9,8},{10,11... | collective-permute-start | bytes 3145736 | tf_op jit(solution)/shard_map/cond/branch_0_fun/ppermute | solution.py:199
  14.1 1.9 %collective-permute-start = (bf16[320,1024]{1,0:T(8,128)(2,1)S(1)}, bf16[320,1024]{1,0:T(8,128)(2,1)S(1)}, u32[]{:S(2)}, u32[]{:S(2)}) collective-permute-start(bf16[320,1024]{1,0:T(8,128)(2,1)S(1)} %pad_maximum_fusion.1), channel_id=1, source_target_pairs={{0,1},{1,0},{2,3},{3,2},{4,5},{5,4},{6,7},{7,6},{8,9},{9,8},{10,11... | collective-permute-start | bytes 1966088 | tf_op jit(solution)/shard_map/cond/branch_0_fun/ppermute | solution.py:199
  16.0 8.7 %collective-permute-start.1 = (bf16[2048,128]{1,0:T(8,128)(2,1)}, bf16[2048,128]{1,0:T(8,128)(2,1)S(1)}, u32[]{:S(2)}, u32[]{:S(2)}) collective-permute-start(bf16[2048,128]{1,0:T(8,128)(2,1)} %bitcast.1.w_key), channel_id=1, source_target_pairs={{0,16},{16,0},{32,48},{48,32},{64,80},{80,64},{96,112},{112,96},{1... | collective-permute-start | bytes 1572872 | tf_op jit(solution)/shard_map/cond/branch_0_fun/ppermute | solution.py:199
  24.7 1.9 %collective-permute-start.2 = (bf16[2048,128]{1,0:T(8,128)(2,1)}, bf16[2048,128]{1,0:T(8,128)(2,1)S(1)}, u32[]{:S(2)}, u32[]{:S(2)}) collective-permute-start(bf16[2048,128]{1,0:T(8,128)(2,1)} %bitcast.2.w_value), channel_id=1, source_target_pairs={{0,16},{16,0},{32,48},{48,32},{64,80},{80,64},{96,112},{112,96},{1... | collective-permute-start | bytes 1572872 | tf_op jit(solution)/shard_map/cond/branch_0_fun/ppermute | solution.py:199
  26.6 2.1 %collective-permute-done.2.value_far = bf16[2048,128]{1,0:T(8,128)(2,1)S(1)} collective-permute-done((bf16[2048,128]{1,0:T(8,128)(2,1)}, bf16[2048,128]{1,0:T(8,128)(2,1)S(1)}, u32[]{:S(2)}, u32[]{:S(2)}) %collective-permute-start.2) | collective-permute-done | bytes 524320 | tf_op jit(solution)/shard_map/cond/branch_0_fun/ppermute | solution.py:199
  29.5 16.5 %collective-permute-done.qdo_other = bf16[320,1024]{1,0:T(8,128)(2,1)S(1)} collective-permute-done((bf16[320,1024]{1,0:T(8,128)(2,1)S(1)}, bf16[320,1024]{1,0:T(8,128)(2,1)S(1)}, u32[]{:S(2)}, u32[]{:S(2)}) %collective-permute-start) | collective-permute-done | bytes 655392 | tf_op jit(solution)/shard_map/cond/branch_0_fun/ppermute | solution.py:199
  46.0 0.8 copy-done.17
  46.8 12.0 %all-gather.6.cloned.1.call-done.blocks = bf16[8,320,512]{2,1,0:T(8,128)(2,1)} async-done(((bf16[1,320,512]{2,1,0:T(8,128)(2,1)}), bf16[8,320,512]{2,1,0:T(8,128)(2,1)}) %all-gather.6.cloned.1.call-update) | async-done | bytes 2621456 | tf_op jit(solution)/shard_map/cond/branch_0_fun/all_gather | solution.py:215
  58.8 4.0 %branch_0_fun.7.kv_own = bf16[320,256]{1,0:T(8,128)(2,1)} custom-call(s32[1]{0:T(128)} %bitcast.place, bf16[8,320,512]{2,1,0:T(8,128)(2,1)} %all-gather.6.cloned.1.call-done.blocks, bf16[2048,256]{1,0:T(8,128)(2,1)} %copy-done.52, bf16[2048,256]{1,0:T(8,128)(2,1)} %collective-permute-done.3.w_other), custom_call_target="tpu_custom_call" | custom-call | flops 671088640 | bytes 2621440 | tf_op jit(solution)/shard_map/cond/branch_0_fun/pallas_call | solution.py:86
  62.8 3.3 %collective-permute-start.4 = (bf16[320,256]{1,0:T(8,128)(2,1)}, bf16[320,256]{1,0:T(8,128)(2,1)S(1)}, u32[]{:S(2)}, u32[]{:S(2)}) collective-permute-start(bf16[320,256]{1,0:T(8,128)(2,1)} %branch_0_fun.7.kv_own), channel_id=1, source_target_pairs={{0,1},{1,0},{2,3},{3,2},{4,5},{5,4},{6,7},{7,6},{8,9},{9,8},{10,11... | collective-permute-start | bytes 491528 | tf_op jit(solution)/shard_map/cond/branch_0_fun/ppermute | solution.py:199
  66.2 3.1 %collective-permute-done.4.kv_other = bf16[320,256]{1,0:T(8,128)(2,1)S(1)} collective-permute-done((bf16[320,256]{1,0:T(8,128)(2,1)}, bf16[320,256]{1,0:T(8,128)(2,1)S(1)}, u32[]{:S(2)}, u32[]{:S(2)}) %collective-permute-start.4) | collective-permute-done | bytes 163872 | tf_op jit(solution)/shard_map/cond/branch_0_fun/ppermute | solution.py:199
  69.3 3.1 %collective-permute-start.5 = (bf16[1,320,512]{2,1,0:T(8,128)(2,1)S(1)}, bf16[1,320,512]{2,1,0:T(8,128)(2,1)S(1)}, u32[]{:S(2)}, u32[]{:S(2)}) collective-permute-start(bf16[1,320,512]{2,1,0:T(8,128)(2,1)S(1)} %get-tuple-element.233), channel_id=1, source_target_pairs={{0,1},{1,0},{2,3},{3,2},{4,5},{5,4},{6,7},{7,6},{8,9},{9,8},{10,11... | collective-permute-start | bytes 983048 | tf_op jit(solution)/shard_map/cond/branch_0_fun/ppermute | solution.py:199
  72.5 2.1 %collective-permute-start.6 = (bf16[1,320,512]{2,1,0:T(8,128)(2,1)S(1)}, bf16[1,320,512]{2,1,0:T(8,128)(2,1)S(1)}, u32[]{:S(2)}, u32[]{:S(2)}) collective-permute-start(bf16[1,320,512]{2,1,0:T(8,128)(2,1)S(1)} %get-tuple-element.232), channel_id=1, source_target_pairs={{0,1},{1,0},{2,3},{3,2},{4,5},{5,4},{6,7},{7,6},{8,9},{9,8},{10,11... | collective-permute-start | bytes 983048 | tf_op jit(solution)/shard_map/cond/branch_0_fun/ppermute | solution.py:199
  74.6 3.1 %collective-permute-start.7 = (bf16[1,320,512]{2,1,0:T(8,128)(2,1)S(1)}, bf16[1,320,512]{2,1,0:T(8,128)(2,1)S(1)}, u32[]{:S(2)}, u32[]{:S(2)}) collective-permute-start(bf16[1,320,512]{2,1,0:T(8,128)(2,1)S(1)} %get-tuple-element.231), channel_id=1, source_target_pairs={{0,1},{1,0},{2,3},{3,2},{4,5},{5,4},{6,7},{7,6},{8,9},{9,8},{10,11... | collective-permute-start | bytes 983048 | tf_op jit(solution)/shard_map/cond/branch_0_fun/ppermute | solution.py:199
  77.8 2.3 %collective-permute-start.8 = (bf16[1,320,512]{2,1,0:T(8,128)(2,1)S(1)}, bf16[1,320,512]{2,1,0:T(8,128)(2,1)S(1)}, u32[]{:S(2)}, u32[]{:S(2)}) collective-permute-start(bf16[1,320,512]{2,1,0:T(8,128)(2,1)S(1)} %get-tuple-element.230), channel_id=1, source_target_pairs={{0,1},{1,0},{2,3},{3,2},{4,5},{5,4},{6,7},{7,6},{8,9},{9,8},{10,11... | collective-permute-start | bytes 983048 | tf_op jit(solution)/shard_map/cond/branch_0_fun/ppermute | solution.py:199
  80.1 5.5 %branch_0_fun.8 = (bf16[320,256]{1,0:T(8,128)(2,1)S(1)}, bf16[320,256]{1,0:T(8,128)(2,1)S(1)}) custom-call(s32[1]{0:T(128)} %bitcast.place, bf16[320,512]{1,0:T(8,128)(2,1)S(1)} %bitcast.81, bf16[320,512]{1,0:T(8,128)(2,1)S(1)} %bitcast.91, bf16[320,1024]{1,0:T(8,128)(2,1)S(1)} %copy-done.18, bf16[320,256]{1,0:T(8,128)(2,1)S(1)} %copy-done.12, ...), custom_call_target="tpu_custom_call" | custom-call | flops 1258291200 | bytes 1966084 | tf_op jit(solution)/shard_map/cond/branch_0_fun/pallas_call | solution.py:38
  86.2 8.1 %collective-permute-start.9 = (bf16[512,256]{1,0:T(8,128)(2,1)S(1)}, bf16[512,256]{1,0:T(8,128)(2,1)S(1)}, u32[]{:S(2)}, u32[]{:S(2)}) collective-permute-start(bf16[512,256]{1,0:T(8,128)(2,1)S(1)} %get-tuple-element.92), channel_id=1, source_target_pairs={{0,16},{16,0},{32,48},{48,32},{64,80},{80,64},{96,112},{112,96},{1... | collective-permute-start | bytes 786440 | tf_op jit(solution)/shard_map/cond/branch_0_fun/ppermute | solution.py:199
  94.8 1.9 %collective-permute-start.10 = (bf16[512,256]{1,0:T(8,128)(2,1)S(1)}, bf16[512,256]{1,0:T(8,128)(2,1)S(1)}, u32[]{:S(2)}, u32[]{:S(2)}) collective-permute-start(bf16[512,256]{1,0:T(8,128)(2,1)S(1)} %get-tuple-element.93), channel_id=1, source_target_pairs={{0,16},{16,0},{32,48},{48,32},{64,80},{80,64},{96,112},{112,96},{1... | collective-permute-start | bytes 786440 | tf_op jit(solution)/shard_map/cond/branch_0_fun/ppermute | solution.py:199
  97.3 4.2 %collective-permute-start.11 = (bf16[512,256]{1,0:T(8,128)(2,1)S(1)}, bf16[512,256]{1,0:T(8,128)(2,1)S(1)}, u32[]{:S(2)}, u32[]{:S(2)}) collective-permute-start(bf16[512,256]{1,0:T(8,128)(2,1)S(1)} %get-tuple-element.94), channel_id=1, source_target_pairs={{0,16},{16,0},{32,48},{48,32},{64,80},{80,64},{96,112},{112,96},{1... | collective-permute-start | bytes 786440 | tf_op jit(solution)/shard_map/cond/branch_0_fun/ppermute | solution.py:199
  102.0 2.9 %collective-permute-start.12 = (bf16[512,256]{1,0:T(8,128)(2,1)S(1)}, bf16[512,256]{1,0:T(8,128)(2,1)S(1)}, u32[]{:S(2)}, u32[]{:S(2)}) collective-permute-start(bf16[512,256]{1,0:T(8,128)(2,1)S(1)} %get-tuple-element.95), channel_id=1, source_target_pairs={{0,16},{16,0},{32,48},{48,32},{64,80},{80,64},{96,112},{112,96},{1... | collective-permute-start | bytes 786440 | tf_op jit(solution)/shard_map/cond/branch_0_fun/ppermute | solution.py:199
  104.9 1.1 collective-permute-done.12.refs_7_
  106.0 3.2 %branch_0_fun.13 = (bf16[1,2048,128]{2,1,0:T(8,128)(2,1)}, bf16[1,2048,128]{2,1,0:T(8,128)(2,1)}, bf16[1,2048,128]{2,1,0:T(8,128)(2,1)}, bf16[1,2048,128]{2,1,0:T(8,128)(2,1)}) custom-call(s32[1]{0:T(128)} %bitcast.place, bf16[2048,128]{1,0:T(8,128)(2,1)} %bitcast.1.w_key, bf16[2048,128]{1,0:T(8,128)(2,1)} %bitcast.2.w_value, ...), custom_call_target="tpu_custom_call" | custom-call | bytes 7340036 | tf_op jit(solution)/shard_map/cond/branch_0_fun/pallas_call | solution.py:38
  (42 shorter events, 3.7 us)
Async XLA Ops:
  7.8 6.1 %copy-start.33 = (bf16[1,320,512]{2,1,0:T(8,128)(2,1)S(1)}, bf16[1,320,512]{2,1,0:T(8,128)(2,1)}, u32[]{:S(2)}) copy-start(bf16[1,320,512]{2,1,0:T(8,128)(2,1)} %get-tuple-element.73) | copy-start | bytes 983044 | tf_op jit(solution)/shard_map/cond
  7.9 50.9 %all-gather.6.cloned.1.call-start = ((), (), s32[]{:S(2)}) async-start(), calls=%async_computation | async-start | bytes 2949120 | tf_op jit(solution)/shard_map/cond/branch_0_fun/all_gather | solution.py:215
  9.9 48.9 %copy-start.52 = (bf16[2048,256]{1,0:T(8,128)(2,1)}, bf16[2048,256]{1,0:T(8,128)(2,1)S(1)}, u32[]{:S(2)}) copy-start(bf16[2048,256]{1,0:T(8,128)(2,1)S(1)} %pad_maximum_fusion.w_own) | copy-start | bytes 3145732 | tf_op jit(solution)/shard_map/cond
  9.9 48.9 %collective-permute-start.3 = (bf16[2048,256]{1,0:T(8,128)(2,1)S(1)}, bf16[2048,256]{1,0:T(8,128)(2,1)}, u32[]{:S(2)}, u32[]{:S(2)}) collective-permute-start(bf16[2048,256]{1,0:T(8,128)(2,1)S(1)} %pad_maximum_fusion.w_own), channel_id=1, source_target_pairs={{0,1},{1,0},{2,3},{3,2},{4,5},{5,4},{6,7},{7,6},{8,9},{9,8},{10,11... | collective-permute-start | bytes 3145736 | tf_op jit(solution)/shard_map/cond/branch_0_fun/ppermute | solution.py:199
  14.1 31.9 %collective-permute-start = (bf16[320,1024]{1,0:T(8,128)(2,1)S(1)}, bf16[320,1024]{1,0:T(8,128)(2,1)S(1)}, u32[]{:S(2)}, u32[]{:S(2)}) collective-permute-start(bf16[320,1024]{1,0:T(8,128)(2,1)S(1)} %pad_maximum_fusion.1), channel_id=1, source_target_pairs={{0,1},{1,0},{2,3},{3,2},{4,5},{5,4},{6,7},{7,6},{8,9},{9,8},{10,11... | collective-permute-start | bytes 1966088 | tf_op jit(solution)/shard_map/cond/branch_0_fun/ppermute | solution.py:199
  16.0 10.6 %collective-permute-start.1 = (bf16[2048,128]{1,0:T(8,128)(2,1)}, bf16[2048,128]{1,0:T(8,128)(2,1)S(1)}, u32[]{:S(2)}, u32[]{:S(2)}) collective-permute-start(bf16[2048,128]{1,0:T(8,128)(2,1)} %bitcast.1.w_key), channel_id=1, source_target_pairs={{0,16},{16,0},{32,48},{48,32},{64,80},{80,64},{96,112},{112,96},{1... | collective-permute-start | bytes 1572872 | tf_op jit(solution)/shard_map/cond/branch_0_fun/ppermute | solution.py:199
  24.7 4.0 %collective-permute-start.2 = (bf16[2048,128]{1,0:T(8,128)(2,1)}, bf16[2048,128]{1,0:T(8,128)(2,1)S(1)}, u32[]{:S(2)}, u32[]{:S(2)}) collective-permute-start(bf16[2048,128]{1,0:T(8,128)(2,1)} %bitcast.2.w_value), channel_id=1, source_target_pairs={{0,16},{16,0},{32,48},{48,32},{64,80},{80,64},{96,112},{112,96},{1... | collective-permute-start | bytes 1572872 | tf_op jit(solution)/shard_map/cond/branch_0_fun/ppermute | solution.py:199
  58.8 10.4 %copy-start = (bf16[8,320,512]{2,1,0:T(8,128)(2,1)S(1)}, bf16[8,320,512]{2,1,0:T(8,128)(2,1)}, u32[]{:S(2)}) copy-start(bf16[8,320,512]{2,1,0:T(8,128)(2,1)} %all-gather.6.cloned.1.call-done.blocks) | copy-start | bytes 7864324 | tf_op jit(solution)/shard_map/cond
  62.8 17.3 %copy-start.12 = (bf16[320,256]{1,0:T(8,128)(2,1)S(1)}, bf16[320,256]{1,0:T(8,128)(2,1)}, u32[]{:S(2)}) copy-start(bf16[320,256]{1,0:T(8,128)(2,1)} %branch_0_fun.7.kv_own) | copy-start | bytes 491524 | tf_op jit(solution)/shard_map/cond
  62.8 6.4 %collective-permute-start.4 = (bf16[320,256]{1,0:T(8,128)(2,1)}, bf16[320,256]{1,0:T(8,128)(2,1)S(1)}, u32[]{:S(2)}, u32[]{:S(2)}) collective-permute-start(bf16[320,256]{1,0:T(8,128)(2,1)} %branch_0_fun.7.kv_own), channel_id=1, source_target_pairs={{0,1},{1,0},{2,3},{3,2},{4,5},{5,4},{6,7},{7,6},{8,9},{9,8},{10,11... | collective-permute-start | bytes 491528 | tf_op jit(solution)/shard_map/cond/branch_0_fun/ppermute | solution.py:199
  66.1 14.0 %copy-start.18 = (bf16[320,1024]{1,0:T(8,128)(2,1)S(1)}, bf16[320,1024]{1,0:T(8,128)(2,1)}, u32[]{:S(2)}) copy-start(bf16[320,1024]{1,0:T(8,128)(2,1)} %copy-done.17) | copy-start | bytes 1966084 | tf_op jit(solution)/shard_map/cond
  66.1 14.0 %copy-start.34 = (bf16[1,320,512]{2,1,0:T(8,128)(2,1)S(1)}, bf16[1,320,512]{2,1,0:T(8,128)(2,1)}, u32[]{:S(2)}) copy-start(bf16[1,320,512]{2,1,0:T(8,128)(2,1)} %get-tuple-element.73) | copy-start | bytes 983044 | tf_op jit(solution)/shard_map/cond
  66.2 14.0 %copy-start.43 = (bf16[1,320,512]{2,1,0:T(8,128)(2,1)S(1)}, bf16[1,320,512]{2,1,0:T(8,128)(2,1)}, u32[]{:S(2)}) copy-start(bf16[1,320,512]{2,1,0:T(8,128)(2,1)} %get-tuple-element.74) | copy-start | bytes 983044 | tf_op jit(solution)/shard_map/cond
  69.3 16.3 %collective-permute-start.5 = (bf16[1,320,512]{2,1,0:T(8,128)(2,1)S(1)}, bf16[1,320,512]{2,1,0:T(8,128)(2,1)S(1)}, u32[]{:S(2)}, u32[]{:S(2)}) collective-permute-start(bf16[1,320,512]{2,1,0:T(8,128)(2,1)S(1)} %get-tuple-element.233), channel_id=1, source_target_pairs={{0,1},{1,0},{2,3},{3,2},{4,5},{5,4},{6,7},{7,6},{8,9},{9,8},{10,11... | collective-permute-start | bytes 983048 | tf_op jit(solution)/shard_map/cond/branch_0_fun/ppermute | solution.py:199
  72.5 21.8 %collective-permute-start.6 = (bf16[1,320,512]{2,1,0:T(8,128)(2,1)S(1)}, bf16[1,320,512]{2,1,0:T(8,128)(2,1)S(1)}, u32[]{:S(2)}, u32[]{:S(2)}) collective-permute-start(bf16[1,320,512]{2,1,0:T(8,128)(2,1)S(1)} %get-tuple-element.232), channel_id=1, source_target_pairs={{0,1},{1,0},{2,3},{3,2},{4,5},{5,4},{6,7},{7,6},{8,9},{9,8},{10,11... | collective-permute-start | bytes 983048 | tf_op jit(solution)/shard_map/cond/branch_0_fun/ppermute | solution.py:199
  74.6 22.1 %collective-permute-start.7 = (bf16[1,320,512]{2,1,0:T(8,128)(2,1)S(1)}, bf16[1,320,512]{2,1,0:T(8,128)(2,1)S(1)}, u32[]{:S(2)}, u32[]{:S(2)}) collective-permute-start(bf16[1,320,512]{2,1,0:T(8,128)(2,1)S(1)} %get-tuple-element.231), channel_id=1, source_target_pairs={{0,1},{1,0},{2,3},{3,2},{4,5},{5,4},{6,7},{7,6},{8,9},{9,8},{10,11... | collective-permute-start | bytes 983048 | tf_op jit(solution)/shard_map/cond/branch_0_fun/ppermute | solution.py:199
  77.8 7.9 %copy-start.23 = (bf16[1,2048,128]{2,1,0:T(8,128)(2,1)S(1)}, bf16[1,2048,128]{2,1,0:T(8,128)(2,1)}, u32[]{:S(2)}) copy-start(bf16[1,2048,128]{2,1,0:T(8,128)(2,1)} %get-tuple-element.86) | copy-start | bytes 1572868 | tf_op jit(solution)/shard_map/cond
  77.8 7.9 %copy-start.28 = (bf16[1,2048,128]{2,1,0:T(8,128)(2,1)S(1)}, bf16[1,2048,128]{2,1,0:T(8,128)(2,1)}, u32[]{:S(2)}) copy-start(bf16[1,2048,128]{2,1,0:T(8,128)(2,1)} %get-tuple-element.87) | copy-start | bytes 1572868 | tf_op jit(solution)/shard_map/cond
  77.8 23.7 %collective-permute-start.8 = (bf16[1,320,512]{2,1,0:T(8,128)(2,1)S(1)}, bf16[1,320,512]{2,1,0:T(8,128)(2,1)S(1)}, u32[]{:S(2)}, u32[]{:S(2)}) collective-permute-start(bf16[1,320,512]{2,1,0:T(8,128)(2,1)S(1)} %get-tuple-element.230), channel_id=1, source_target_pairs={{0,1},{1,0},{2,3},{3,2},{4,5},{5,4},{6,7},{7,6},{8,9},{9,8},{10,11... | collective-permute-start | bytes 983048 | tf_op jit(solution)/shard_map/cond/branch_0_fun/ppermute | solution.py:199
  86.2 18.6 %collective-permute-start.9 = (bf16[512,256]{1,0:T(8,128)(2,1)S(1)}, bf16[512,256]{1,0:T(8,128)(2,1)S(1)}, u32[]{:S(2)}, u32[]{:S(2)}) collective-permute-start(bf16[512,256]{1,0:T(8,128)(2,1)S(1)} %get-tuple-element.92), channel_id=1, source_target_pairs={{0,16},{16,0},{32,48},{48,32},{64,80},{80,64},{96,112},{112,96},{1... | collective-permute-start | bytes 786440 | tf_op jit(solution)/shard_map/cond/branch_0_fun/ppermute | solution.py:199
  94.8 10.0 %collective-permute-start.10 = (bf16[512,256]{1,0:T(8,128)(2,1)S(1)}, bf16[512,256]{1,0:T(8,128)(2,1)S(1)}, u32[]{:S(2)}, u32[]{:S(2)}) collective-permute-start(bf16[512,256]{1,0:T(8,128)(2,1)S(1)} %get-tuple-element.93), channel_id=1, source_target_pairs={{0,16},{16,0},{32,48},{48,32},{64,80},{80,64},{96,112},{112,96},{1... | collective-permute-start | bytes 786440 | tf_op jit(solution)/shard_map/cond/branch_0_fun/ppermute | solution.py:199
  97.3 8.7 %copy-start.6 = (bf16[2048,128]{1,0:T(8,128)(2,1)S(1)}, bf16[2048,128]{1,0:T(8,128)(2,1)}, u32[]{:S(2)}) copy-start(bf16[2048,128]{1,0:T(8,128)(2,1)} %copy-done.5) | copy-start | bytes 1572868 | tf_op jit(solution)/shard_map/cond
  97.3 7.6 %collective-permute-start.11 = (bf16[512,256]{1,0:T(8,128)(2,1)S(1)}, bf16[512,256]{1,0:T(8,128)(2,1)S(1)}, u32[]{:S(2)}, u32[]{:S(2)}) collective-permute-start(bf16[512,256]{1,0:T(8,128)(2,1)S(1)} %get-tuple-element.94), channel_id=1, source_target_pairs={{0,16},{16,0},{32,48},{48,32},{64,80},{80,64},{96,112},{112,96},{1... | collective-permute-start | bytes 786440 | tf_op jit(solution)/shard_map/cond/branch_0_fun/ppermute | solution.py:199
  102.0 4.0 %collective-permute-start.12 = (bf16[512,256]{1,0:T(8,128)(2,1)S(1)}, bf16[512,256]{1,0:T(8,128)(2,1)S(1)}, u32[]{:S(2)}, u32[]{:S(2)}) collective-permute-start(bf16[512,256]{1,0:T(8,128)(2,1)S(1)} %get-tuple-element.95), channel_id=1, source_target_pairs={{0,16},{16,0},{32,48},{48,32},{64,80},{80,64},{96,112},{112,96},{1... | collective-permute-start | bytes 786440 | tf_op jit(solution)/shard_map/cond/branch_0_fun/ppermute | solution.py:199
  (3 other events, 7.8 us)
Sparse Core Ops, SparseCore 0:
  10.8 47.9 all-gather.5
